TPU v7x, 32 devices: a whole 2x2x4 slice. The times are simulated.
32 devices in a mesh: dp: 16 (over z, y, x), tensor: 2 (over core).
Axes of the slice: x: 2, y: 2, z: 4, core: 2. Of those that a mesh axis runs over, the one named last changes fastest.
Arguments:
- latents: bfloat16 [16, 1184, 1536], P('dp', 'tensor'), may hold values from -6 to 6
- conditioning: bfloat16 [16, 1536], P('dp'), may hold values from -6 to 6
- valid_length: int32 [16], P('dp'), may hold values from 1025 to 1178, as said below
- cotangent: bfloat16 [16, 1184, 1536], P('dp', 'tensor'), may hold values from -6 to 6
- modulation: float32 [2, 1536, 9216], P(None, 'dp', 'tensor'), may hold values from -0.15625 to 0.15625
- attention: float32 [2, 1536, 3, 1536], P(None, 'dp', None, 'tensor'), may hold values from -0.15625 to 0.15625
- outward: float32 [2, 1536, 1536], P(None, 'tensor', 'dp'), may hold values from -1.25 to 1.25
- expand: float32 [2, 1536, 6144], P(None, 'dp', 'tensor'), may hold values from -0.15625 to 0.15625
- shrink: float32 [2, 6144, 1536], P(None, 'tensor', 'dp'), may hold values from -0.078125 to 0.078125
- modulation_moment: float32 [2, 1536, 9216], P(None, 'dp', 'tensor'), may hold values from -7104 to 7104
- attention_moment: float32 [2, 1536, 3, 1536], P(None, 'dp', None, 'tensor'), may hold values from -7104 to 7104
- outward_moment: float32 [2, 1536, 1536], P(None, 'tensor', 'dp'), may hold values from -6 to 6
- expand_moment: float32 [2, 1536, 6144], P(None, 'dp', 'tensor'), may hold values from -6 to 6
- shrink_moment: float32 [2, 6144, 1536], P(None, 'tensor', 'dp'), may hold values from -6 to 6
- modulation_average: float32 [2, 1536, 9216], P(None, 'dp', 'tensor'), may hold values from -0.15625 to 0.15625
- attention_average: float32 [2, 1536, 3, 1536], P(None, 'dp', None, 'tensor'), may hold values from -0.15625 to 0.15625
- outward_average: float32 [2, 1536, 1536], P(None, 'tensor', 'dp'), may hold values from -1.25 to 1.25
- expand_average: float32 [2, 1536, 6144], P(None, 'dp', 'tensor'), may hold values from -0.15625 to 0.15625
- shrink_average: float32 [2, 6144, 1536], P(None, 'tensor', 'dp'), may hold values from -0.078125 to 0.078125
Outputs:
- block_output: bfloat16 [16, 1184, 1536], P('dp', 'tensor')
- input_gradient: float32 [16, 1184, 1536], P('dp', 'tensor')
- conditioning_gradient: float32 [16, 1536], P('dp', 'tensor')
- modulation_updated: float32 [2, 1536, 9216], P(None, 'dp', 'tensor')
- modulation_momentum: float32 [2, 1536, 9216], P(None, 'dp', 'tensor')
- modulation_smoothed: float32 [2, 1536, 9216], P(None, 'dp', 'tensor')
- attention_updated: float32 [2, 1536, 3, 1536], P(None, 'dp', None, 'tensor')
- attention_momentum: float32 [2, 1536, 3, 1536], P(None, 'dp', None, 'tensor')
- attention_smoothed: float32 [2, 1536, 3, 1536], P(None, 'dp', None, 'tensor')
- outward_updated: float32 [2, 1536, 1536], P(None, 'tensor', 'dp')
- outward_momentum: float32 [2, 1536, 1536], P(None, 'tensor', 'dp')
- outward_smoothed: float32 [2, 1536, 1536], P(None, 'tensor', 'dp')
- expand_updated: float32 [2, 1536, 6144], P(None, 'dp', 'tensor')
- expand_momentum: float32 [2, 1536, 6144], P(None, 'dp', 'tensor')
- expand_smoothed: float32 [2, 1536, 6144], P(None, 'dp', 'tensor')
- shrink_updated: float32 [2, 6144, 1536], P(None, 'tensor', 'dp')
- shrink_momentum: float32 [2, 6144, 1536], P(None, 'tensor', 'dp')
- shrink_smoothed: float32 [2, 6144, 1536], P(None, 'tensor', 'dp')
Inputs may be any that keep to these rules, and one draw needn't show every extreme that they name: `valid_length`: 1024 image tokens plus a count of valid text tokens; among the one consecutive sequence one has all 154 text tokens valid.
All inputs are finite; a program needn't handle non-finite values.
Results may differ from a plain program's by a relative error of at most 0.018.
The roundings to bfloat16 on the way count: a program that leaves them out, or rounds other values in their place, can miss the bound.
Values may be sent and summed in bfloat16 or wider, within the bound.
No kernel may reach another device: no remote copies, remote signals or barrier semaphores. Data moves between devices by JAX's collectives and lax.ppermute only.
A program may use at most 512 MiB of HBM per device.

v0:
```python
from functools import partial
import math

import jax
import jax.numpy as jnp
from jax import lax
from jax.sharding import PartitionSpec as P

HEAD = 64
IMG = 1024


EPSILON = 1e-06
RATE = 0.0005
MOMENTUM = 0.9
AVERAGING = 0.8
MASKED = -1000000000.0


def layer_norm(values):
    center = values - jnp.mean(values, axis=-1, keepdims=True)
    spread = jnp.mean(center * center, axis=-1, keepdims=True)
    return center * lax.rsqrt(spread + EPSILON)


def stream_dot(rows, weight):
    image = jnp.einsum("slk,km->slm", rows[:, :IMG], weight[0], preferred_element_type=jnp.float32)
    text = jnp.einsum("slk,km->slm", rows[:, IMG:], weight[1], preferred_element_type=jnp.float32)
    return jnp.concatenate([image, text], axis=1)


def stream_back(rows, weight):
    image = jnp.einsum("slm,km->slk", rows[:, :IMG], weight[0], preferred_element_type=jnp.float32)
    text = jnp.einsum("slm,km->slk", rows[:, IMG:], weight[1], preferred_element_type=jnp.float32)
    return jnp.concatenate([image, text], axis=1)


def stream_outer(left, right):
    image = jnp.einsum(
        "slk,slm->km", left[:, :IMG], right[:, :IMG], preferred_element_type=jnp.float32
    )
    text = jnp.einsum(
        "slk,slm->km", left[:, IMG:], right[:, IMG:], preferred_element_type=jnp.float32
    )
    return jnp.stack([image, text])


def masked_scores(query, keys, length, scale):
    allowed = jnp.arange(keys.shape[0]) < length
    raw = jnp.einsum("qhe,khe->hqk", query, keys, preferred_element_type=jnp.float32) * scale
    return jnp.where(allowed[None, None, :], raw, MASKED)


def attend_forward(item, scale):
    query, keys, values, length = item
    scores = masked_scores(query, keys, length, scale)
    peak = jnp.max(scores, axis=-1, keepdims=True)
    expo = jnp.exp(scores - peak)
    total = jnp.sum(expo, axis=-1, keepdims=True)
    probs = (expo / total).astype(jnp.bfloat16)
    mixed = jnp.einsum("hqk,khe->qhe", probs, values, preferred_element_type=jnp.float32)
    return (mixed.astype(jnp.bfloat16), (peak + jnp.log(total))[..., 0])


def attend_backward(item, scale):
    query, keys, values, length, logsum, upstream = item
    scores = masked_scores(query, keys, length, scale)
    probs = jnp.exp(scores - logsum[..., None])
    dprobs = jnp.einsum("qhe,khe->hqk", upstream, values, preferred_element_type=jnp.float32)
    inner = jnp.sum(probs * dprobs, axis=-1, keepdims=True)
    dscores = (probs * (dprobs - inner)).astype(jnp.bfloat16)
    query_grad = (
        jnp.einsum("hqk,khe->qhe", dscores, keys, preferred_element_type=jnp.float32) * scale
    )
    key_grad = (
        jnp.einsum("hqk,qhe->khe", dscores, query, preferred_element_type=jnp.float32) * scale
    )
    value_grad = jnp.einsum(
        "hqk,qhe->khe", probs.astype(jnp.bfloat16), upstream, preferred_element_type=jnp.float32
    )
    return (
        query_grad.astype(jnp.bfloat16),
        key_grad.astype(jnp.bfloat16),
        value_grad.astype(jnp.bfloat16),
    )


def per_device(
    latents,
    conditioning,
    valid_length,
    cotangent,
    modulation,
    attention,
    outward,
    expand,
    shrink,
    modulation_moment,
    attention_moment,
    outward_moment,
    expand_moment,
    shrink_moment,
    modulation_average,
    attention_average,
    outward_average,
    expand_average,
    shrink_average,
):
    local_rows = latents.shape[1]
    width = latents.shape[2]
    heads_here = attention.shape[3] // HEAD
    scale = 1.0 / math.sqrt(HEAD)
    masters = (modulation, attention, outward, expand, shrink)
    moments = (modulation_moment, attention_moment, outward_moment, expand_moment, shrink_moment)
    averages = (
        modulation_average,
        attention_average,
        outward_average,
        expand_average,
        shrink_average,
    )
    mod_low = modulation.astype(jnp.bfloat16)
    attn_low = attention.astype(jnp.bfloat16)
    out_low = outward.astype(jnp.bfloat16)
    expand_low = expand.astype(jnp.bfloat16)
    shrink_low = shrink.astype(jnp.bfloat16)
    cond_value = conditioning.astype(jnp.float32)
    silu_cond, silu_pull = jax.vjp(jax.nn.silu, cond_value)
    cond_low = silu_cond.astype(jnp.bfloat16)
    gathered = (
        lax.all_gather(mod_low, "dp", axis=1, tiled=True),
        lax.all_gather(attn_low, "dp", axis=1, tiled=True),
        lax.all_gather(out_low, "dp", axis=2, tiled=True),
        lax.all_gather(expand_low, "dp", axis=1, tiled=True),
        lax.all_gather(shrink_low, "dp", axis=2, tiled=True),
    )
    mod_part = jnp.einsum("sd,idm->ism", cond_low, gathered[0], preferred_element_type=jnp.float32)
    mods = lax.all_gather(mod_part, "tensor", axis=2, tiled=True)
    positions = lax.axis_index("tensor") * local_rows + jnp.arange(local_rows)
    image_rows = (positions < IMG)[None, :, None]
    image_mask = image_rows.astype(jnp.float32)

    def component(index):
        image = mods[0][:, None, index * width : (index + 1) * width]
        text = mods[1][:, None, index * width : (index + 1) * width]
        return jnp.where(image_rows, image, text)

    shift_one, scale_one, gate_one, shift_two, scale_two, gate_two = [
        component(index) for index in range(6)
    ]
    residual = latents.astype(jnp.float32)
    normed_one, norm_pull_one = jax.vjp(layer_norm, residual)
    shaped_one = (normed_one * (1.0 + scale_one) + shift_one).astype(jnp.bfloat16)
    rows_one = lax.all_gather(shaped_one, "tensor", axis=1, tiled=True)
    packed = stream_dot(rows_one, gathered[1].reshape(2, width, -1)).astype(jnp.bfloat16)
    seqs_here = packed.shape[0]
    full_len = packed.shape[1]
    split = packed.reshape(seqs_here, full_len, 3, heads_here, HEAD)
    queries, keys_all, values_all = (split[:, :, 0], split[:, :, 1], split[:, :, 2])
    attended, logsums = lax.map(
        partial(attend_forward, scale=scale), (queries, keys_all, values_all, valid_length)
    )
    mixed = attended.reshape(seqs_here, full_len, heads_here * HEAD)
    branch_one = lax.psum_scatter(
        stream_dot(mixed, gathered[2]), "tensor", scatter_dimension=1, tiled=True
    )
    middle = residual + gate_one * branch_one
    normed_two, norm_pull_two = jax.vjp(layer_norm, middle)
    shaped_two = (normed_two * (1.0 + scale_two) + shift_two).astype(jnp.bfloat16)
    rows_two = lax.all_gather(shaped_two, "tensor", axis=1, tiled=True)
    hidden_pre = stream_dot(rows_two, gathered[3])
    hidden_act, gelu_pull = jax.vjp(partial(jax.nn.gelu, approximate=True), hidden_pre)
    hidden_low = hidden_act.astype(jnp.bfloat16)
    branch_two = lax.psum_scatter(
        stream_dot(hidden_low, gathered[4]).astype(jnp.bfloat16),
        "tensor",
        scatter_dimension=1,
        tiled=True,
    ).astype(jnp.float32)
    block_output = (middle + gate_two * branch_two).astype(jnp.bfloat16)
    weights_back = (
        lax.all_gather(mod_low, "dp", axis=1, tiled=True),
        lax.all_gather(attn_low, "dp", axis=1, tiled=True),
        lax.all_gather(out_low, "dp", axis=2, tiled=True),
        lax.all_gather(expand_low, "dp", axis=1, tiled=True),
        lax.all_gather(shrink_low, "dp", axis=2, tiled=True),
    )
    upstream = cotangent.astype(jnp.float32)
    gate_two_grad = upstream * branch_two
    down_in = (gate_two * upstream).astype(jnp.bfloat16)
    down_rows = lax.all_gather(down_in, "tensor", axis=1, tiled=True)
    shrink_grad = stream_outer(hidden_low, down_rows)
    hidden_grad = gelu_pull(stream_back(down_rows, weights_back[4]))[0].astype(jnp.bfloat16)
    expand_grad = stream_outer(rows_two, hidden_grad)
    shaped_two_grad = lax.psum_scatter(
        stream_back(hidden_grad, weights_back[3]), "tensor", scatter_dimension=1, tiled=True
    )
    scale_two_grad = shaped_two_grad * normed_two
    middle_grad = upstream + norm_pull_two(shaped_two_grad * (1.0 + scale_two))[0]
    gate_one_grad = middle_grad * branch_one
    proj_in = (gate_one * middle_grad).astype(jnp.bfloat16)
    proj_rows = lax.all_gather(proj_in, "tensor", axis=1, tiled=True)
    outward_grad = stream_outer(mixed, proj_rows)
    mixed_grad = stream_back(proj_rows, weights_back[2]).astype(jnp.bfloat16)
    mixed_grad = mixed_grad.reshape(seqs_here, full_len, heads_here, HEAD)
    query_grad, key_grad, value_grad = lax.map(
        partial(attend_backward, scale=scale),
        (queries, keys_all, values_all, valid_length, logsums, mixed_grad),
    )
    packed_grad = jnp.stack([query_grad, key_grad, value_grad], axis=2).reshape(
        seqs_here, full_len, -1
    )
    attention_grad = stream_outer(rows_one, packed_grad).reshape(2, width, 3, -1)
    shaped_one_grad = lax.psum_scatter(
        stream_back(packed_grad, weights_back[1].reshape(2, width, -1)).astype(jnp.bfloat16),
        "tensor",
        scatter_dimension=1,
        tiled=True,
    ).astype(jnp.float32)
    latent_grad = middle_grad + norm_pull_one(shaped_one_grad * (1.0 + scale_one))[0]
    pieces = (
        shaped_one_grad,
        shaped_one_grad * normed_one,
        gate_one_grad,
        shaped_two_grad,
        scale_two_grad,
        gate_two_grad,
    )
    image_part = jnp.concatenate([jnp.sum(piece * image_mask, axis=1) for piece in pieces], axis=1)
    text_part = jnp.concatenate(
        [jnp.sum(piece * (1.0 - image_mask), axis=1) for piece in pieces], axis=1
    )
    mod_columns = lax.psum_scatter(
        jnp.stack([image_part, text_part]).astype(jnp.bfloat16),
        "tensor",
        scatter_dimension=2,
        tiled=True,
    ).astype(jnp.float32)
    modulation_grad = jnp.einsum(
        "sd,ism->idm", cond_low.astype(jnp.float32), mod_columns, precision=lax.Precision.HIGHEST
    )
    cond_mine = jnp.einsum(
        "ism,idm->sd",
        mod_columns,
        weights_back[0].astype(jnp.float32),
        precision=lax.Precision.HIGHEST,
    )
    reduced = (
        lax.psum_scatter(
            modulation_grad.astype(jnp.bfloat16), "dp", scatter_dimension=1, tiled=True
        ).astype(jnp.float32),
        lax.psum_scatter(
            attention_grad.astype(jnp.bfloat16), "dp", scatter_dimension=1, tiled=True
        ).astype(jnp.float32),
        lax.psum_scatter(
            outward_grad.astype(jnp.bfloat16), "dp", scatter_dimension=2, tiled=True
        ).astype(jnp.float32),
        lax.psum_scatter(
            expand_grad.astype(jnp.bfloat16), "dp", scatter_dimension=1, tiled=True
        ).astype(jnp.float32),
        lax.psum_scatter(
            shrink_grad.astype(jnp.bfloat16), "dp", scatter_dimension=2, tiled=True
        ).astype(jnp.float32),
    )
    cond_part = silu_pull(cond_mine)[0]
    conditioning_grad = lax.psum_scatter(cond_part, "tensor", scatter_dimension=1, tiled=True)
    results = [block_output, latent_grad, conditioning_grad]
    for master, moment, average, summed in zip(masters, moments, averages, reduced):
        velocity = MOMENTUM * moment + summed
        updated = master - RATE * (summed + MOMENTUM * velocity)
        smoothed = AVERAGING * average + (1.0 - AVERAGING) * updated
        results += [updated, velocity, smoothed]
    return tuple(results)


def solution(mesh):
    return jax.shard_map(
        per_device,
        mesh=mesh,
        in_specs=(
            P("dp", "tensor", None),
            P("dp", None),
            P("dp"),
            P("dp", "tensor", None),
            P(None, "dp", "tensor"),
            P(None, "dp", None, "tensor"),
            P(None, "tensor", "dp"),
            P(None, "dp", "tensor"),
            P(None, "tensor", "dp"),
            P(None, "dp", "tensor"),
            P(None, "dp", None, "tensor"),
            P(None, "tensor", "dp"),
            P(None, "dp", "tensor"),
            P(None, "tensor", "dp"),
            P(None, "dp", "tensor"),
            P(None, "dp", None, "tensor"),
            P(None, "tensor", "dp"),
            P(None, "dp", "tensor"),
            P(None, "tensor", "dp"),
        ),
        out_specs=(
            P("dp", "tensor", None),
            P("dp", "tensor", None),
            P("dp", "tensor"),
            P(None, "dp", "tensor"),
            P(None, "dp", "tensor"),
            P(None, "dp", "tensor"),
            P(None, "dp", None, "tensor"),
            P(None, "dp", None, "tensor"),
            P(None, "dp", None, "tensor"),
            P(None, "tensor", "dp"),
            P(None, "tensor", "dp"),
            P(None, "tensor", "dp"),
            P(None, "dp", "tensor"),
            P(None, "dp", "tensor"),
            P(None, "dp", "tensor"),
            P(None, "tensor", "dp"),
            P(None, "tensor", "dp"),
            P(None, "tensor", "dp"),
        ),
        check_vma=False,
    )
```

profile of v0, /device:TPU:0, one launch (start us, length us, event | category | flops | bytes accessed | tf_op | source)
XLA Modules:
  0.0 3136.3 jit_solution(6678592618195135185)
XLA Ops:
  15.7 299.7 %all-gather.11.cloned.1.call-done = bf16[2,1536,4608]{2,1,0:T(8,128)(2,1)} async-done(((bf16[2,96,4608]{2,1,0:T(8,128)(2,1)}), bf16[2,1536,4608]{2,1,0:T(8,128)(2,1)}) %all-gather.11.cloned.1.call-update) | async-done | bytes 28311568 | tf_op jit(solution)/shard_map/all_gather | solution.py:131
  334.1 149.7 %all-gather.15.cloned.1.call-done = bf16[2,1536,3,768]{3,0,2,1:T(2,128)(2,1)} async-done(((bf16[2,96,3,768]{3,0,2,1:T(2,128)(2,1)}), bf16[2,1536,3,768]{3,0,2,1:T(2,128)(2,1)}) %all-gather.15.cloned.1.call-update) | async-done | bytes 14155792 | tf_op jit(solution)/shard_map/all_gather | solution.py:132
  483.8 28.2 fusion.153
  512.0 33.1 %copy.135 = bf16[1,1536,3,768]{1,3,2,0:T(8,128)(2,1)} copy(bf16[1,1536,3,768]{3,0,2,1:T(2,128)(2,1)} %get-tuple-element.178) | data formatting | bytes 14155776
  545.1 33.0 %copy.136 = bf16[1,1536,3,768]{1,3,2,0:T(8,128)(2,1)} copy(bf16[1,1536,3,768]{3,0,2,1:T(2,128)(2,1)} %get-tuple-element.179) | data formatting | bytes 14155776
  594.1 28.8 fusion.155
  622.9 22.9 fusion.1
  645.8 27.0 fusion.56
  704.3 208.8 %all-gather.23.cloned.1.call-done = bf16[2,3072,1536]{1,2,0:T(8,128)(2,1)} async-done(((bf16[2,3072,96]{1,2,0:T(8,128)(2,1)}), bf16[2,3072,1536]{1,2,0:T(8,128)(2,1)}) %all-gather.23.cloned.1.call-update) | async-done | bytes 18874384 | tf_op jit(solution)/shard_map/all_gather | solution.py:135
  932.0 15.3 fusion.27
  947.3 195.0 %all-gather.21.cloned.1.call-done = bf16[2,1536,3072]{2,1,0:T(8,128)(2,1)} async-done(((bf16[2,96,3072]{2,1,0:T(8,128)(2,1)}), bf16[2,1536,3072]{2,1,0:T(8,128)(2,1)}) %all-gather.21.cloned.1.call-update) | async-done | bytes 18874384 | tf_op jit(solution)/shard_map/all_gather | solution.py:134
  1155.5 16.0 fusion.28
  1287.4 47.0 %multiply_reduce_fusion = (f32[12,1184]{1,0:T(8,128)S(1)}, f32[12,1184,1184]{1,2,0:T(8,128)}) fusion(f32[12,1184,1184]{1,2,0:T(8,128)} %get-tuple-element.186, f32[12,1184]{1,0:T(8,128)S(1)} %log_add_fusion, bf16[1,1024,3,12,64]{1,4,3,2,0:T(8,128)(2,1)} %convert_bitcast_fusion.2, bf16[1,160,3,12,64]{1,4,3,2,0:T(8,128)(2,1)S(1)} %copy-done.9, ...), kind=kOutput, calls=%fused_computation.3 | convolution fusion | flops 2210977792 | bytes 141966336 | tf_op jit(solution)/shard_map/while/body/eval_jaxpr/qhe,khe->hqk/dot_general | solution.py:69
  1334.4 57.7 %multiply_convert_fusion = bf16[12,1184,1184]{1,2,0:T(8,128)(2,1)} fusion(f32[12,1184,1184]{1,2,0:T(8,128)} %get-tuple-element.188, f32[12,1184,1184]{1,2,0:T(8,128)} %get-tuple-element.186, f32[12,1184]{1,0:T(8,128)S(1)} %get-tuple-element.187, f32[12,1184]{1,0:T(8,128)S(1)} %log_add_fusion), kind=kLoop, calls=%fused_computation.2 | loop fusion | flops 67289088 | bytes 168336384 | tf_op jit(solution)/shard_map/while/body/eval_jaxpr/convert_element_type | solution.py:71
  1392.1 19.5 fusion.80
  1411.6 18.3 fusion.79
  1429.8 25.5 fusion.72
  1474.6 15.7 fusion.15
  1558.3 16.6 pad_maximum_fusion
  1600.3 47.2 %copy.118 = bf16[2,3072,1536]{1,0,2:T(2,128)(2,1)} copy(bf16[2,3072,1536]{2,1,0:T(8,128)(2,1)} %pad_maximum_fusion.1) | data formatting | bytes 37748736 | tf_op jit(solution)/shard_map/stack | solution.py:45
  1717.5 144.3 %reduce-scatter.26.cloned.1.call-done = bf16[2,96,3072]{2,1,0:T(8,128)(2,1)} async-done(((bf16[2,1536,3072]{2,1,0:T(8,128)(2,1)}), bf16[2,96,3072]{2,1,0:T(8,128)(2,1)}) %reduce-scatter.26.cloned.1.call-update) | async-done | bytes 1179664 | tf_op jit(solution)/shard_map/reduce_scatter | solution.py:258
  1869.2 620.2 %all-reduce.5.cloned.1.call-done = (bf16[2,768,1536]{1,0,2:T(2,128)(2,1)}, bf16[2,3072,1536]{1,0,2:T(2,128)(2,1)}) async-done(((bf16[2,768,1536]{1,0,2:T(2,128)(2,1)}, bf16[2,3072,1536]{1,0,2:T(2,128)(2,1)}), (bf16[2,768,1536]{1,0,2:T(2,128)(2,1)}, bf16[2,3072,1536]{1,0,2:T(2,128)(2,1)})) %all-reduce.5.cloned.1.call-update) | async-done | bytes 23592976
  2500.9 215.5 %reduce-scatter.24.cloned.1.call-done = bf16[2,96,3,768]{3,1,2,0:T(8,128)(2,1)} async-done(((bf16[2,1536,3,768]{3,1,2,0:T(8,128)(2,1)}), bf16[2,96,3,768]{3,1,2,0:T(8,128)(2,1)}) %reduce-scatter.24.cloned.1.call-update) | async-done | bytes 884752 | tf_op jit(solution)/shard_map/reduce_scatter | solution.py:252
  2722.0 398.5 %reduce-scatter.22.cloned.1.call-done = bf16[2,96,4608]{2,1,0:T(8,128)(2,1)} async-done(((bf16[2,1536,4608]{2,1,0:T(8,128)(2,1)}), bf16[2,96,4608]{2,1,0:T(8,128)(2,1)}) %reduce-scatter.22.cloned.1.call-update) | async-done | bytes 1769488 | tf_op jit(solution)/shard_map/reduce_scatter | solution.py:249
  (281 shorter events, 436.5 us)
Async XLA Ops:
  7.2 308.2 %all-gather.11.cloned.1.call-start = ((), (), s32[]{:S(2)}) async-start(), calls=%async_computation.9 | async-start | bytes 30081024 | tf_op jit(solution)/shard_map/all_gather | solution.py:131
  10.7 473.2 %all-gather.15.cloned.1.call-start = ((), (), s32[]{:S(2)}) async-start(), calls=%async_computation.11 | async-start | bytes 15040512 | tf_op jit(solution)/shard_map/all_gather | solution.py:132
  14.6 563.5 %all-gather.13.cloned.1.call-start = ((), (), s32[]{:S(2)}) async-start(), calls=%async_computation.10 | async-start | bytes 5455872 | tf_op jit(solution)/shard_map/all_gather | solution.py:154
  14.7 314.5 %copy-start.30 = (pred[592]{0:T(1024)(128)(4,1)}, pred[592]{0:T(1024)(128)(4,1)S(1)}, u32[]{:S(2)}) copy-start(pred[592]{0:T(1024)(128)(4,1)S(1)} %add_compare_fusion) | copy-start | bytes 1780
  332.1 340.6 %all-gather.17.cloned.1.call-start = ((), (), s32[]{:S(2)}) async-start(), calls=%async_computation.12 | async-start | bytes 5013504 | tf_op jit(solution)/shard_map/all_gather | solution.py:133
  332.9 364.4 %reduce-scatter.14.cloned.1.call-start = ((), (), s32[]{:S(2)}) async-start(), calls=%async_computation.13 | async-start | bytes 10911744 | tf_op jit(solution)/shard_map/reduce_scatter | solution.py:164
  683.1 230.0 %all-gather.23.cloned.1.call-start = ((), (), s32[]{:S(2)}) async-start(), calls=%async_computation.16 | async-start | bytes 20054016 | tf_op jit(solution)/shard_map/all_gather | solution.py:135
  686.0 240.3 %all-gather.25.cloned.1.call-start = ((), (), s32[]{:S(2)}) async-start(), calls=%async_computation.18 | async-start | bytes 5455872 | tf_op jit(solution)/shard_map/all_gather | solution.py:191
  686.7 455.5 %all-gather.21.cloned.1.call-start = ((), (), s32[]{:S(2)}) async-start(), calls=%async_computation.15 | async-start | bytes 20054016 | tf_op jit(solution)/shard_map/all_gather | solution.py:134
  690.3 465.1 %all-gather.19.cloned.1.call-start = ((), (), s32[]{:S(2)}) async-start(), calls=%async_computation.14 | async-start | bytes 5455872 | tf_op jit(solution)/shard_map/all_gather | solution.py:170
  704.3 537.6 %reduce-scatter.18.cloned.1.call-start = ((), (), s32[]{:S(2)}) async-start(), calls=%async_computation.19 | async-start | bytes 10911744 | tf_op jit(solution)/shard_map/reduce_scatter | solution.py:195
  1219.6 34.8 %reduce-scatter.16.cloned.1.call-start = ((), (), s32[]{:S(2)}) async-start(), calls=%async_computation.17 | async-start | bytes 5455872 | tf_op jit(solution)/shard_map/reduce_scatter | solution.py:174
  1241.6 37.4 %all-gather.27.cloned.1.call-start = ((), (), s32[]{:S(2)}) async-start(), calls=%async_computation.20 | async-start | bytes 5455872 | tf_op jit(solution)/shard_map/all_gather | solution.py:202
  1264.8 225.5 %reduce-scatter.20.cloned.1.call-start = ((), (), s32[]{:S(2)}) async-start(), calls=%async_computation.21 | async-start | bytes 5455872 | tf_op jit(solution)/shard_map/reduce_scatter | solution.py:214
  1474.5 53.1 %reduce-scatter.28.cloned.1.call-start = ((), (), s32[]{:S(2)}) async-start(), calls=%async_computation.25 | async-start | bytes 3538944
  1516.4 199.3 %reduce-scatter.30.cloned.1.call-start = ((), (), s32[]{:S(2)}) async-start(), calls=%async_computation.26 | async-start | bytes 1179648
  1558.3 303.5 %reduce-scatter.26.cloned.1.call-start = ((), (), s32[]{:S(2)}) async-start(), calls=%async_computation.24 | async-start | bytes 20054016 | tf_op jit(solution)/shard_map/reduce_scatter | solution.py:258
  1574.9 914.5 %all-reduce.5.cloned.1.call-start = ((), (), s32[]{:S(2)}) async-start(), calls=%async_computation.27 | async-start | bytes 47185920
  1669.6 1046.7 %reduce-scatter.24.cloned.1.call-start = ((), (), s32[]{:S(2)}) async-start(), calls=%async_computation.23 | async-start | bytes 15040512 | tf_op jit(solution)/shard_map/reduce_scatter | solution.py:252
  1698.0 1422.5 %reduce-scatter.22.cloned.1.call-start = ((), (), s32[]{:S(2)}) async-start(), calls=%async_computation.22 | async-start | bytes 30081024 | tf_op jit(solution)/shard_map/reduce_scatter | solution.py:249
  1717.5 773.3 %copy-start.19 = (f32[2,768,96]{1,2,0:T(8,128)S(1)}, f32[2,768,96]{1,2,0:T(8,128)}, u32[]{:S(2)}) copy-start(f32[2,768,96]{1,2,0:T(8,128)} %param.25) | copy-start | bytes 1769476
  1717.5 773.3 %copy-start.21 = (f32[2,768,96]{1,2,0:T(8,128)S(1)}, f32[2,768,96]{1,2,0:T(8,128)}, u32[]{:S(2)}) copy-start(f32[2,768,96]{1,2,0:T(8,128)} %param.35) | copy-start | bytes 1769476
  1869.2 626.1 %copy-start.15 = (f32[2,3072,96]{1,2,0:T(8,128)S(1)}, f32[2,3072,96]{1,2,0:T(8,128)}, u32[]{:S(2)}) copy-start(f32[2,3072,96]{1,2,0:T(8,128)} %param.27) | copy-start | bytes 7077892
  2500.9 619.7 %copy-start.12 = (f32[2,96,4608]{2,1,0:T(8,128)S(1)}, f32[2,96,4608]{2,1,0:T(8,128)}, u32[]{:S(2)}) copy-start(f32[2,96,4608]{2,1,0:T(8,128)} %param.23) | copy-start | bytes 10616836
  (59 other events, 1707.3 us)
Sparse Core Ops, SparseCore 0:
  11.3 304.0 all-gather.10
  318.7 165.0 all-gather.14
  485.9 11.0 all-gather.12
  500.1 81.7 all-gather.16
  683.2 14.0 reduce-scatter.13
  700.4 212.6 all-gather.22
  915.2 11.0 all-gather.24
  929.6 212.6 all-gather.20
  1144.4 11.0 all-gather.18
  1219.7 16.9 reduce-scatter.17
  1241.7 12.6 reduce-scatter.15
  1264.9 14.0 all-gather.26
  1474.6 12.6 reduce-scatter.19
  1516.6 11.0 reduce-scatter.27
  1558.4 9.3 reduce-scatter.29
  1575.0 286.7 reduce-scatter.25
  1868.1 621.3 all-reduce.4
  2496.0 220.2 reduce-scatter.23
  2722.1 398.3 reduce-scatter.21
where the time goes:
time: 3150 us; the launch traced here: 3140 us
  waiting for transfers between devices  2280 us (72%)
  matrix products  381 us (12%)
  other arithmetic  236 us (7%)
  local copies, waits for them, and re-layouts  220 us (7%)
    unnamed x22, waiting for transfers between devices  624 us
    reduce_scatter x1, waiting for transfers between devices, per_device(): lax.psum_scatter(modulation_grad.astype(jnp.bfloat16), 'dp', scatter_dime...  399 us
    all_gather x1, waiting for transfers between devices, per_device(): lax.all_gather(mod_low, 'dp', axis=1, tiled=True)  300 us
    reduce_scatter x1, waiting for transfers between devices, per_device(): lax.psum_scatter(attention_grad.astype(jnp.bfloat16), 'dp', scatter_dimen...  215 us
    all_gather x1, waiting for transfers between devices, per_device(): lax.all_gather(shrink_low, 'dp', axis=2, tiled=True)  209 us
    all_gather x1, waiting for transfers between devices, per_device(): lax.all_gather(expand_low, 'dp', axis=1, tiled=True)  195 us
    all_gather x1, waiting for transfers between devices, per_device(): lax.all_gather(attn_low, 'dp', axis=1, tiled=True)  150 us
    reduce_scatter x1, waiting for transfers between devices, per_device(): lax.psum_scatter(expand_grad.astype(jnp.bfloat16), 'dp', scatter_dimensio...  144 us
  transfers between devices with their start and end apart: 19, of which 14 were waited for; matrix products, arithmetic and copies ran while one was open for 15% of the time, Pallas kernels for 0%

commit v1 on v0

v1 whole, which is shorter than its diff:
```python
from functools import partial
import math

import jax
import jax.numpy as jnp
from jax import lax
from jax.experimental import pallas as pl
from jax.experimental.pallas import tpu as pltpu
from jax.sharding import PartitionSpec as P

HEAD = 64
IMG = 1024


EPSILON = 1e-06
RATE = 0.0005
MOMENTUM = 0.9
AVERAGING = 0.8
MASKED = -1000000000.0
TILE = 256
PAIR = 2 * HEAD

F32 = jnp.float32
BF16 = jnp.bfloat16


def mm(left, right):
    return lax.dot_general(left, right, (((1,), (0,)), ((), ())), preferred_element_type=F32)


def mm_nt(left, right):
    return lax.dot_general(left, right, (((1,), (1,)), ((), ())), preferred_element_type=F32)


def mm_tn(left, right):
    return lax.dot_general(left, right, (((0,), (0,)), ((), ())), preferred_element_type=F32)


def fill(scratch, image_ref, text_ref):
    text = text_ref.shape[0]
    scratch[pl.ds(0, IMG), :] = image_ref[...]
    scratch[pl.ds(IMG, text), :] = text_ref[...]
    rest = scratch.shape[0] - IMG - text
    if rest:
        scratch[pl.ds(IMG + text, rest), :] = jnp.zeros((rest, scratch.shape[1]), scratch.dtype)


def open_slots(length, shape, axis):
    return lax.broadcasted_iota(jnp.int32, shape, axis) + IMG < length


def forward_kernel(sequence, length_ref, qi, ki, vi, qt, kt, vt, oi, ot, lse_ref, q_s, k_s, v_s, o_s):
    rows = q_s.shape[0]
    fill(q_s, qi, qt)
    fill(k_s, ki, kt)
    fill(v_s, vi, vt)
    lane = lax.broadcasted_iota(jnp.int32, (1, PAIR), 1)
    open_slot = open_slots(length_ref[sequence], (TILE, rows - IMG), 1)

    def one_tile(step, carry):
        start = pl.multiple_of(step * TILE, TILE)
        query = q_s[pl.ds(start, TILE), :]
        out = jnp.zeros((TILE, PAIR), F32)
        for half in range(2):
            mine = (lane // HEAD) == half
            mine_query = jnp.where(mine, query * 0.125, jnp.zeros_like(query))
            image = mm_nt(mine_query, k_s[pl.ds(0, IMG), :])
            text = mm_nt(mine_query, k_s[pl.ds(IMG, rows - IMG), :])
            text = jnp.where(open_slot, text, MASKED)
            peak = jnp.maximum(
                jnp.max(image, axis=1, keepdims=True), jnp.max(text, axis=1, keepdims=True)
            )
            image = jnp.exp(image - peak)
            text = jnp.exp(text - peak)
            total = jnp.sum(image, axis=1, keepdims=True) + jnp.sum(text, axis=1, keepdims=True)
            mixed = mm(image.astype(BF16), v_s[pl.ds(0, IMG), :])
            mixed += mm(text.astype(BF16), v_s[pl.ds(IMG, rows - IMG), :])
            out = jnp.where(mine, mixed * (1.0 / total), out)
            wide = jnp.broadcast_to(peak + jnp.log(total), (TILE, 128))
            lse_ref[0, pl.ds(half, 1), pl.ds(start, TILE)] = wide.T[:1]
        o_s[pl.ds(start, TILE), :] = out.astype(BF16)
        return carry

    lax.fori_loop(0, rows // TILE, one_tile, 0)
    oi[...] = o_s[pl.ds(0, IMG), :]
    ot[...] = o_s[pl.ds(IMG, ot.shape[0]), :]


def backward_kernel(
    sequence, length_ref, qi, ki, vi, di, qt, kt, vt, dt, lse_ref, gi, gt, q_s, k_s, v_s, d_s, kt_s, dq_s, dk_s, dv_s
):
    rows = q_s.shape[0]
    which = pl.program_id(1)

    @pl.when(which == 0)
    def compute():
        fill(q_s, qi, qt)
        fill(k_s, ki, kt)
        fill(v_s, vi, vt)
        fill(d_s, di, dt)
        kt_s[...] = k_s[...].T
        dk_s[...] = jnp.zeros_like(dk_s)
        dv_s[...] = jnp.zeros_like(dv_s)
        lane = lax.broadcasted_iota(jnp.int32, (1, PAIR), 1)
        open_slot = open_slots(length_ref[sequence], (rows - IMG, TILE), 0)

        def one_tile(step, carry):
            start = pl.multiple_of(step * TILE, TILE)
            query = q_s[pl.ds(start, TILE), :]
            upper = d_s[pl.ds(start, TILE), :]
            pieces = []
            for half in range(2):
                mine = (lane // HEAD) == half
                mine_query = jnp.where(mine, query * 0.125, jnp.zeros_like(query))
                mine_upper = jnp.where(mine, upper, jnp.zeros_like(upper))
                logsum = lse_ref[0, pl.ds(half, 1), pl.ds(start, TILE)]
                image = mm_nt(k_s[pl.ds(0, IMG), :], mine_query)
                text = mm_nt(k_s[pl.ds(IMG, rows - IMG), :], mine_query)
                text = jnp.where(open_slot, text, MASKED)
                image = jnp.exp(image - logsum)
                text = jnp.exp(text - logsum)
                up_image = mm_nt(v_s[pl.ds(0, IMG), :], mine_upper)
                up_text = mm_nt(v_s[pl.ds(IMG, rows - IMG), :], mine_upper)
                inner = jnp.sum(image * up_image, axis=0, keepdims=True)
                inner += jnp.sum(text * up_text, axis=0, keepdims=True)
                dv_s[pl.ds(0, IMG), :] += mm(image.astype(BF16), mine_upper)
                dv_s[pl.ds(IMG, rows - IMG), :] += mm(text.astype(BF16), mine_upper)
                d_image = (image * (up_image - inner)).astype(BF16)
                d_text = (text * (up_text - inner)).astype(BF16)
                dk_s[pl.ds(0, IMG), :] += mm(d_image, mine_query)
                dk_s[pl.ds(IMG, rows - IMG), :] += mm(d_text, mine_query)
                keys = kt_s[pl.ds(half * HEAD, HEAD), :]
                pieces.append(mm(keys[:, :IMG], d_image) + mm(keys[:, IMG:], d_text))
            across = jnp.concatenate(pieces, axis=0) * 0.125
            dq_s[pl.ds(start, TILE), :] = across.T.astype(BF16)
            return carry

        lax.fori_loop(0, rows // TILE, one_tile, 0)

    text_rows = gt.shape[0]

    @pl.when(which == 0)
    def write_query():
        gi[...] = dq_s[pl.ds(0, IMG), :]
        gt[...] = dq_s[pl.ds(IMG, text_rows), :]

    @pl.when(which == 1)
    def write_key():
        gi[...] = dk_s[pl.ds(0, IMG), :].astype(BF16)
        gt[...] = dk_s[pl.ds(IMG, text_rows), :].astype(BF16)

    @pl.when(which == 2)
    def write_value():
        gi[...] = dv_s[pl.ds(0, IMG), :].astype(BF16)
        gt[...] = dv_s[pl.ds(IMG, text_rows), :].astype(BF16)


def padded_rows(text):
    return -(-(IMG + text) // TILE) * TILE


def attend_forward(packed_image, packed_text, lengths, sequence):
    text = packed_text.shape[0]
    pairs = packed_image.shape[1] // (3 * PAIR)
    rows = padded_rows(text)

    def block(height, part):
        return pl.BlockSpec((height, PAIR), lambda j, _: (0, part * pairs + j))

    def result(height):
        return pl.BlockSpec((height, PAIR), lambda j, _: (0, j))

    return pl.pallas_call(
        partial(forward_kernel, sequence),
        grid_spec=pltpu.PrefetchScalarGridSpec(
            num_scalar_prefetch=1,
            grid=(pairs,),
            in_specs=[block(IMG, part) for part in range(3)]
            + [block(text, part) for part in range(3)],
            out_specs=[
                result(IMG),
                result(text),
                pl.BlockSpec((1, 2, rows), lambda j, _: (j, 0, 0)),
            ],
            scratch_shapes=[pltpu.VMEM((rows, PAIR), BF16)] * 4,
        ),
        out_shape=[
            jax.ShapeDtypeStruct((IMG, pairs * PAIR), BF16),
            jax.ShapeDtypeStruct((text, pairs * PAIR), BF16),
            jax.ShapeDtypeStruct((pairs, 2, rows), F32),
        ],
        compiler_params=pltpu.CompilerParams(vmem_limit_bytes=48 * 1024 * 1024),
        cost_estimate=pl.CostEstimate(
            flops=16 * pairs * rows * rows * PAIR,
            bytes_accessed=8 * pairs * rows * PAIR,
            transcendentals=2 * pairs * rows * rows,
        ),
        name="attend_forward",
    )(lengths, *([packed_image] * 3), *([packed_text] * 3))


def attend_backward(packed_image, packed_text, up_image, up_text, logsums, lengths, sequence):
    text = up_text.shape[0]
    pairs = packed_image.shape[1] // (3 * PAIR)
    rows = padded_rows(text)

    def block(height, part):
        return pl.BlockSpec((height, PAIR), lambda j, c, _: (0, part * pairs + j))

    def upper(height):
        return pl.BlockSpec((height, PAIR), lambda j, c, _: (0, j))

    return pl.pallas_call(
        partial(backward_kernel, sequence),
        grid_spec=pltpu.PrefetchScalarGridSpec(
            num_scalar_prefetch=1,
            grid=(pairs, 3),
            in_specs=[block(IMG, part) for part in range(3)]
            + [upper(IMG)]
            + [block(text, part) for part in range(3)]
            + [upper(text)]
            + [pl.BlockSpec((1, 2, rows), lambda j, c, _: (j, 0, 0))],
            out_specs=[
                pl.BlockSpec((IMG, PAIR), lambda j, c, _: (0, c * pairs + j)),
                pl.BlockSpec((text, PAIR), lambda j, c, _: (0, c * pairs + j)),
            ],
            scratch_shapes=[pltpu.VMEM((rows, PAIR), BF16)] * 4
            + [
                pltpu.VMEM((PAIR, rows), BF16),
                pltpu.VMEM((rows, PAIR), BF16),
                pltpu.VMEM((rows, PAIR), F32),
                pltpu.VMEM((rows, PAIR), F32),
            ],
        ),
        out_shape=[
            jax.ShapeDtypeStruct((IMG, 3 * pairs * PAIR), BF16),
            jax.ShapeDtypeStruct((text, 3 * pairs * PAIR), BF16),
        ],
        compiler_params=pltpu.CompilerParams(vmem_limit_bytes=48 * 1024 * 1024),
        cost_estimate=pl.CostEstimate(
            flops=40 * pairs * rows * rows * PAIR,
            bytes_accessed=16 * pairs * rows * PAIR,
            transcendentals=2 * pairs * rows * rows,
        ),
        name="attend_backward",
    )(
        lengths,
        *([packed_image] * 3),
        up_image,
        *([packed_text] * 3),
        up_text,
        logsums,
    )


def swap(values):
    return lax.ppermute(values, "tensor", [(0, 1), (1, 0)])


def tensor_gather(values, size, axis):
    if size == 2:
        other = swap(values)
        return jnp.where(
            lax.axis_index("tensor") == 0,
            jnp.concatenate([values, other], axis=axis),
            jnp.concatenate([other, values], axis=axis),
        )
    return lax.all_gather(values, "tensor", axis=axis, tiled=True)


def tensor_sum(values, size):
    if size == 2:
        return values + swap(values)
    return lax.psum(values, "tensor")


def tensor_scatter(image, text, size):
    values = jnp.concatenate([image, text], axis=0)
    rows = values.shape[0] // size
    if size == 2:
        me = lax.axis_index("tensor")
        away = lax.dynamic_slice_in_dim(values, (1 - me) * rows, rows, 0).astype(BF16)
        return lax.dynamic_slice_in_dim(values, me * rows, rows, 0) + swap(away).astype(F32)
    return lax.psum_scatter(values, "tensor", scatter_dimension=0, tiled=True)


def bit(k):
    return (lax.axis_index("dp") >> k) & 1


def flip(values, bits, groups):
    return lax.ppermute(values, "dp", [(index, index ^ bits) for index in range(groups)])


def over_pair(values, groups):
    return flip(values, 1, groups)


def count_bits(groups):
    return groups.bit_length() - 1


def small_order(groups):
    return [0] + list(range(count_bits(groups) - 1, 0, -1))


def small_gather(block, groups):
    for k in small_order(groups):
        block = jnp.concatenate([block, flip(block, 1 << k, groups)], axis=0)
    return block


def small_scatter(values, groups, pair):
    for k in reversed(small_order(groups)[1 if pair else 0 :]):
        half = values.shape[0] // 2
        values = values[:half] + flip(values[half:], 1 << k, groups)
    if pair:
        got = over_pair(values, groups)
        values = values + jnp.concatenate([got[1:], got[:1]], axis=0)
    return values


def same_side(groups):
    return [[index for index in range(groups) if index % 2 == side] for side in range(2)]


def pair_rows(image, text, kinds, groups):
    def halves(shard):
        return shard.reshape(shard.shape[0], kinds, 2, -1)

    split = jnp.concatenate([halves(image), halves(text)], axis=1)

    def side(which):
        part = lax.dynamic_index_in_dim(split, which, 2, keepdims=False)
        return part.reshape(part.shape[0], -1).astype(BF16)

    return side(bit(0)), over_pair(side(1 - bit(0)), groups)


def pair_join(mine, got):
    first = bit(0) == 0
    return jnp.concatenate([jnp.where(first, mine, got), jnp.where(first, got, mine)], axis=0)


def pair_gather(rows, groups):
    return lax.all_gather(rows, "dp", axis=0, tiled=True, axis_index_groups=same_side(groups))


def streams_of(weight):
    half = weight.shape[1] // 2
    return weight[:, :half], weight[:, half:]


def adjacent(first, second):
    return jnp.concatenate([first, second], axis=1)


def pair_scatter(grads, groups):
    return lax.psum_scatter(
        grads,
        "dp",
        scatter_dimension=0,
        tiled=True,
        axis_index_groups=same_side(groups),
    )


def own_shard(pair, kinds, groups):
    share = pair.shape[0] // 2
    mine = lax.dynamic_slice_in_dim(pair, bit(0) * share, share, 0)
    got = over_pair(lax.dynamic_slice_in_dim(pair, (1 - bit(0)) * share, share, 0), groups)
    first = bit(0) == 0
    halves = [jnp.where(first, mine, got), jnp.where(first, got, mine)]
    split = [half.reshape(share, 2, kinds, -1) for half in halves]
    return jnp.stack(split, axis=3).reshape(share, 2, -1).transpose(1, 0, 2).astype(F32)


def phase(*values):
    return lax.optimization_barrier(values)


def normalize(values):
    center = values - jnp.mean(values, axis=-1, keepdims=True)
    spread = jnp.mean(center * center, axis=-1, keepdims=True)
    scale = lax.rsqrt(spread + EPSILON)
    return center * scale, scale


def norm_back(normed, scale, grad):
    inner = jnp.mean(grad * normed, axis=-1, keepdims=True)
    return (grad - jnp.mean(grad, axis=-1, keepdims=True) - normed * inner) * scale


ROOT = math.sqrt(2.0 / math.pi)


def gelu_both(value):
    curve = jnp.tanh(ROOT * (value + 0.044715 * value * value * value))
    act = 0.5 * value * (1.0 + curve)
    slope = 0.5 * (1.0 + curve) + 0.5 * value * (1.0 - curve * curve) * ROOT * (
        1.0 + 3.0 * 0.044715 * value * value
    )
    return act, slope


def per_device(
    sizes,
    latents,
    conditioning,
    valid_length,
    cotangent,
    modulation,
    attention,
    outward,
    expand,
    shrink,
    modulation_moment,
    attention_moment,
    outward_moment,
    expand_moment,
    shrink_moment,
    modulation_average,
    attention_average,
    outward_average,
    expand_average,
    shrink_average,
):
    groups, tensors = sizes
    local_rows = latents.shape[1]
    width = latents.shape[2]
    share = width // groups
    heads_here = attention.shape[3] // HEAD
    spare = -heads_here % 4 * HEAD
    me_dp = lax.axis_index("dp")
    me_tensor = lax.axis_index("tensor")
    masters = (modulation, attention, outward, expand, shrink)
    moments = (modulation_moment, attention_moment, outward_moment, expand_moment, shrink_moment)
    averages = (
        modulation_average,
        attention_average,
        outward_average,
        expand_average,
        shrink_average,
    )

    def more_heads(values):
        return jnp.pad(values, ((0, 0),) * (values.ndim - 1) + ((0, spare),)) if spare else values

    def cut(local):
        rows = tensor_gather(local, tensors, 0)
        return rows[:IMG], rows[IMG:]

    attn_rows = pair_rows(more_heads(attention[0]), more_heads(attention[1]), 3, groups)
    out_rows = pair_rows(more_heads(outward[0].T), more_heads(outward[1].T), 1, groups)
    lengths = jnp.concatenate(
        [valid_length, over_pair(valid_length.astype(F32), groups).astype(jnp.int32)]
    )

    cond_value = conditioning.astype(F32)
    silu_cond, silu_pull = jax.vjp(jax.nn.silu, cond_value)
    cond_block = silu_cond.astype(BF16).reshape(1, -1, 128)
    cond_all = small_gather(cond_block, groups).reshape(groups, width)
    lengths, attn_rows, out_rows, cond_all = phase(lengths, attn_rows, out_rows, cond_all)
    heads_whole = pair_gather(adjacent(pair_join(*attn_rows), pair_join(*out_rows)), groups)
    cond_cols = lax.dynamic_slice_in_dim(cond_all, me_dp * share, share, 1)
    mod_low = modulation.astype(BF16)
    columns = modulation.shape[2]
    mod_part = jnp.einsum("sd,idm->sim", cond_cols, mod_low, preferred_element_type=F32)
    mod_sum = small_scatter(mod_part.reshape(groups, -1, 128), groups, True)
    mod_sum, latents_other = phase(mod_sum, over_pair(phase(latents[0], cond_all)[0], groups))
    expand_shards = phase(expand, mod_sum)[0]
    shrink_shards = phase(shrink, mod_sum)[0]
    expand_rows = pair_rows(expand_shards[0], expand_shards[1], 1, groups)
    shrink_rows = pair_rows(shrink_shards[0].T, shrink_shards[1].T, 1, groups)

    mods = tensor_gather(mod_sum.reshape(2, 2, columns), tensors, 2).reshape(2, 2, 6, width)
    both = range(2)
    image_row = me_tensor * local_rows + jnp.arange(local_rows)[:, None] < IMG
    here = [jnp.where(image_row, mods[0, 0, c][None], mods[0, 1, c][None]) for c in range(6)]
    residual, upstream = latents[0].astype(F32), cotangent[0].astype(F32)

    rows_one, packed = [], []
    for q, local in enumerate((latents[0], latents_other)):
        shaped = [
            normalize(rows.astype(F32))[0] * (1.0 + mods[q, i, 1]) + mods[q, i, 0]
            for i, rows in enumerate(cut(local))
        ]
        rows_one.append([values.astype(BF16) for values in shaped])
    rows_one, expand_rows, shrink_rows, upstream_other = phase(
        rows_one, expand_rows, shrink_rows, over_pair(phase(cotangent[0], mod_sum)[0], groups)
    )
    expand_whole = pair_gather(pair_join(*expand_rows), groups)
    shrink_whole = pair_gather(pair_join(*shrink_rows), groups)
    columns_q = 3 * (heads_here * HEAD + spare) // 2
    attn_w = streams_of(heads_whole[:, : 2 * columns_q])
    out_w = streams_of(heads_whole[:, 2 * columns_q :])
    packed = [[mm(rows_one[q][i], attn_w[i]).astype(BF16) for i in both] for q in both]

    *mixed_other, logs_other = attend_forward(*packed[1], lengths, 1)
    away = tensor_scatter(*[mm_nt(mixed_other[i], out_w[i]) for i in both], tensors).astype(BF16)
    away, packed[0] = phase(away, packed[0])
    down_in = []
    for q, local in enumerate((cotangent[0], upstream_other)):
        down = [mods[q, i, 5] * rows.astype(F32) for i, rows in enumerate(cut(local))]
        down_in.append([values.astype(BF16) for values in down])
    (*mixed_own, logs_own), away, down_in = phase(
        attend_forward(*packed[0], lengths, 0), over_pair(away, groups), down_in
    )

    branch_one = tensor_scatter(*[mm_nt(mixed_own[i], out_w[i]) for i in both], tensors)
    branch_one = branch_one + away.astype(F32)
    middle = residual + here[2] * branch_one
    normed_two, inv_two = normalize(middle)
    rows_two = (normed_two * (1.0 + here[4]) + here[3]).astype(BF16)

    def hidden_units(rows, weight):
        act, slope = gelu_both(mm(rows, weight))
        return act.astype(BF16), slope.astype(BF16)

    def hidden_back(down, weight, slope):
        return (mm(down, weight) * slope.astype(F32)).astype(BF16)

    expand_w = streams_of(expand_whole)
    rows_own = cut(rows_two)
    hidden_own = [hidden_units(rows_own[i], expand_w[i]) for i in both]
    shrink_own = [mm_tn(down_in[0][i], hidden_own[i][0]) for i in both]
    hidden_own, shrink_own, rows_other = phase(
        hidden_own, shrink_own, over_pair(rows_two, groups)
    )
    rows_other = cut(rows_other)
    hidden_other = [hidden_units(rows_other[i], expand_w[i]) for i in both]
    shrink_grad = [
        (shrink_own[i] + mm_tn(down_in[1][i], hidden_other[i][0])).astype(BF16) for i in both
    ]

    shrink_grad, hidden_own, hidden_other, shrink_whole = phase(
        shrink_grad, hidden_own, hidden_other, shrink_whole
    )
    shrink_w = streams_of(shrink_whole)
    shrink_sum = pair_scatter(adjacent(*shrink_grad), groups)

    back_other = [hidden_back(down_in[1][i], shrink_w[i], hidden_other[i][1]) for i in both]
    away = tensor_scatter(*[mm_nt(back_other[i], expand_w[i]) for i in both], tensors).astype(BF16)
    back_own = [hidden_back(down_in[0][i], shrink_w[i], hidden_own[i][1]) for i in both]
    back_own, back_other, away = phase(back_own, back_other, away)
    two_grad = tensor_scatter(*[mm_nt(back_own[i], expand_w[i]) for i in both], tensors)
    expand_grad = [
        (mm_tn(rows_own[i], back_own[i]) + mm_tn(rows_other[i], back_other[i])).astype(BF16)
        for i in both
    ]
    branch_away = tensor_scatter(
        *[mm_nt(hidden_other[i][0], shrink_w[i]) for i in both], tensors
    ).astype(BF16)
    two_grad, expand_grad, branch_away, away = phase(
        two_grad, expand_grad, branch_away, over_pair(away, groups)
    )
    expand_sum = pair_scatter(adjacent(*expand_grad), groups)
    two_grad = two_grad + away.astype(F32)
    middle_grad = upstream + norm_back(normed_two, inv_two, two_grad * (1.0 + here[4]))
    proj_in = (here[2] * middle_grad).astype(BF16)

    proj_own = cut(proj_in)
    mixed_grad = [mm(proj_own[i], out_w[i]).astype(BF16) for i in both]
    mixed_grad, proj_in = phase(mixed_grad, proj_in)
    grad_own, proj_other = phase(
        attend_backward(*packed[0], *mixed_grad, logs_own, lengths, 0),
        over_pair(proj_in, groups),
    )
    proj_other = cut(proj_other)
    mixed_grad = [mm(proj_other[i], out_w[i]).astype(BF16) for i in both]
    heads_own = [mm_tn(rows_one[0][i], grad_own[i]) for i in both]
    outward_grad = [
        (mm_tn(proj_own[i], mixed_own[i]) + mm_tn(proj_other[i], mixed_other[i])).astype(BF16)
        for i in both
    ]
    mixed_grad, branch_away, heads_own, outward_grad = phase(
        mixed_grad, branch_away, heads_own, outward_grad
    )
    grad_other, branch_away = phase(
        attend_backward(*packed[1], *mixed_grad, logs_other, lengths, 1),
        over_pair(branch_away, groups),
    )

    heads_grad = [
        (heads_own[i] + mm_tn(rows_one[1][i], grad_other[i])).astype(BF16) for i in both
    ]
    heads_grad = jnp.concatenate(
        [heads_grad[0], outward_grad[0], heads_grad[1], outward_grad[1]], axis=1
    )
    heads_grad, grad_other, grad_own, hidden_own = phase(
        heads_grad, grad_other, grad_own, hidden_own
    )
    heads_sum = pair_scatter(heads_grad, groups)
    away = tensor_scatter(*[mm_nt(grad_other[i], attn_w[i]) for i in both], tensors).astype(BF16)
    away, grad_own, hidden_own = phase(away, grad_own, hidden_own)
    one_grad = tensor_scatter(*[mm_nt(grad_own[i], attn_w[i]) for i in both], tensors)
    branch_two = tensor_scatter(*[mm_nt(hidden_own[i][0], shrink_w[i]) for i in both], tensors)
    branch_two = branch_two + branch_away.astype(F32)
    block_output = (middle + here[5] * branch_two).astype(BF16)
    one_grad, branch_two, away = phase(one_grad, branch_two, over_pair(away, groups))
    one_grad = one_grad + away.astype(F32)
    normed_one, inv_one = normalize(residual)
    latent_grad = middle_grad + norm_back(normed_one, inv_one, one_grad * (1.0 + here[1]))

    pieces = (
        one_grad,
        one_grad * normed_one,
        middle_grad * branch_one,
        two_grad,
        two_grad * normed_two,
        upstream * branch_two,
    )
    mod_grad = [jnp.sum(jnp.where(image_row, piece, 0.0), axis=0) for piece in pieces]
    mod_grad += [jnp.sum(jnp.where(image_row, 0.0, piece), axis=0) for piece in pieces]
    mod_grad = tensor_sum(jnp.stack(mod_grad), tensors).reshape(2, 6 * width)
    mod_columns = lax.dynamic_slice_in_dim(mod_grad, me_tensor * columns, columns, 1)
    mod_columns = mod_columns.astype(BF16).reshape(1, -1, 128)
    all_columns = small_gather(mod_columns, groups).astype(F32).reshape(groups, 2, columns)
    modulation_grad = jnp.einsum(
        "sd,sim->idm", cond_cols.astype(F32), all_columns, precision=lax.Precision.HIGHEST
    )
    cond_part = jnp.einsum(
        "sim,idm->sd", all_columns, mod_low.astype(F32), precision=lax.Precision.HIGHEST
    )
    cond_part = tensor_sum(cond_part, tensors)
    cond_wide = lax.dynamic_update_slice_in_dim(
        jnp.zeros((groups, width), F32), cond_part, me_dp * share, 1
    )
    cond_mine = small_scatter(cond_wide.reshape(groups, -1, 128), groups, False)
    cond_grad = silu_pull(cond_mine.reshape(1, width))[0]
    cond_share = width // tensors
    conditioning_grad = lax.dynamic_slice_in_dim(cond_grad, me_tensor * cond_share, cond_share, 1)

    shrink_grads = own_shard(shrink_sum, 1, groups).transpose(0, 2, 1)
    expand_grads = own_shard(expand_sum, 1, groups)
    heads_grads = own_shard(heads_sum, 4, groups).reshape(2, share, 4, -1)[..., : heads_here * HEAD]
    reduced = (
        modulation_grad,
        heads_grads[:, :, :3],
        heads_grads[:, :, 3].transpose(0, 2, 1),
        expand_grads,
        shrink_grads,
    )
    results = [block_output[None], latent_grad[None], conditioning_grad]
    for master, moment, average, summed in zip(masters, moments, averages, reduced):
        velocity = MOMENTUM * moment + summed
        updated = master - RATE * (summed + MOMENTUM * velocity)
        smoothed = AVERAGING * average + (1.0 - AVERAGING) * updated
        results += [updated, velocity, smoothed]
    return tuple(results)


def solution(mesh):
    tokens = P("dp", "tensor", None)
    by_rows = P(None, "dp", "tensor")
    by_heads = P(None, "dp", None, "tensor")
    by_columns = P(None, "tensor", "dp")
    weights = (by_rows, by_heads, by_columns, by_rows, by_columns)
    return jax.shard_map(
        partial(per_device, (mesh.shape["dp"], mesh.shape["tensor"])),
        mesh=mesh,
        in_specs=(tokens, P("dp", None), P("dp"), tokens) + 3 * weights,
        out_specs=(tokens, tokens, P("dp", "tensor"))
        + tuple(spec for spec in weights for _ in range(3)),
        check_vma=False,
    )
```

time: 3150 us -> 1060 us (0.34)
  waiting for transfers between devices: 2280 us -> 356 us
  matrix products: 381 us -> 235 us
  local copies, waits for them, and re-layouts: 220 us -> 74.2 us
  Pallas kernels: 0 us -> 132 us
  starting transfers between devices: 1.43 us -> 43.2 us
  other arithmetic: 236 us -> 198 us
    all_gather x9 -> x3, waiting for transfers between devices: 883 us -> 69.1 us  [pair_gather(): lax.all_gather(rows, 'dp', axis=0, tiled=True, axis_index_groups=same_sid...]
    reduce_scatter x7 -> x3, waiting for transfers between devices: 772 us -> 41.6 us  [pair_scatter(): lax.psum_scatter(grads, 'dp', scatter_dimension=0, tiled=True, axis_index...]
    unnamed x22 -> x6, waiting for transfers between devices: 624 us -> 0.1 us
    ppermute x0 -> x51, waiting for transfers between devices: none -> 245 us  [the longest x32 226 us: flip(): lax.ppermute(values, 'dp', [(index, index ^ bits) for index in range(grou...]
    dot_general x32 -> x51, matrix products: 381 us -> 235 us  [the longest x16 74.2 us: mm(): lax.dot_general(left, right, (((1,), (0,)), ((), ())), preferred_element_...]
    pallas_call x0 -> x4, Pallas kernels: none -> 132 us  [the longest x2 85.7 us: attend_backward(): pl.pallas_call(partial(backward_kernel, sequence), grid_spec=pltpu.Prefet...]
    unnamed x150 -> x226, local copies, waits for them, and re-layouts: 114 us -> 17.8 us
    another operation x2 -> x33, local copies, waits for them, and re-layouts: 59.9 us -> 15.5 us  [the longest x8 10 us: halves(): return shard.reshape(shard.shape[0], kinds, 2, -1)]
  transfers between devices with their start and end apart: 19 -> 57, of which waited for: 14 -> 33; matrix products, arithmetic and copies ran while one was open for 15% -> 44% of each run, Pallas kernels for 0% -> 12%
where the time goes in v1:
time: 1060 us
  waiting for transfers between devices  356 us (34%)
  matrix products  235 us (22%)
  other arithmetic  198 us (19%)
  Pallas kernels  132 us (12%)
  local copies, waits for them, and re-layouts  74.2 us (7%)
  starting transfers between devices  43.2 us (4%)
  between operations  18.3 us (2%)
    ppermute x32, waiting for transfers between devices, flip(): lax.ppermute(values, 'dp', [(index, index ^ bits) for index in range(grou...  226 us
    pallas_call x2, Pallas kernels, attend_backward(): pl.pallas_call(partial(backward_kernel, sequence), grid_spec=pltpu.Prefet...  85.7 us
    dot_general x16, matrix products, mm(): lax.dot_general(left, right, (((1,), (0,)), ((), ())), preferred_element_...  74.2 us
    dot_general x16, matrix products, mm_nt(): lax.dot_general(left, right, (((1,), (1,)), ((), ())), preferred_element_...  73.7 us
    dot_general x16, matrix products, mm_tn(): lax.dot_general(left, right, (((0,), (0,)), ((), ())), preferred_element_...  72.2 us
    all_gather x3, waiting for transfers between devices, pair_gather(): lax.all_gather(rows, 'dp', axis=0, tiled=True, axis_index_groups=same_sid...  69.1 us
    pallas_call x2, Pallas kernels, attend_forward(): pl.pallas_call(partial(forward_kernel, sequence), grid_spec=pltpu.Prefetc...  46 us
    reduce_scatter x3, waiting for transfers between devices, pair_scatter(): lax.psum_scatter(grads, 'dp', scatter_dimension=0, tiled=True, axis_index...  41.6 us
  transfers between devices with their start and end apart: 57, of which 33 were waited for; matrix products, arithmetic and copies ran while one was open for 44% of the time, Pallas kernels for 12%

profile of v1, /device:TPU:0, one launch (start us, length us, event | category | flops | bytes accessed | tf_op | source)
XLA Modules:
  0.0 1056.0 jit_solution(17001752391542946297)
XLA Ops:
  40.8 9.0 collective-permute-done.7
  50.3 18.5 %collective-permute-done.8 = f32[4,72,128]{2,1,0:T(8,128)S(1)} collective-permute-done((f32[4,72,128]{2,1,0:T(8,128)S(1)}, f32[4,72,128]{2,1,0:T(8,128)S(1)}, u32[]{:S(2)}, u32[]{:S(2)}) %collective-permute-start.8) | collective-permute-done | bytes 147488 | tf_op jit(solution)/shard_map/ppermute | solution.py:292
  69.0 10.5 collective-permute-done.9
  89.1 33.9 %collective-permute-done.11 = bf16[592,1536]{1,0:T(8,128)(2,1)} collective-permute-done((bf16[592,1536]{1,0:T(8,128)(2,1)S(1)}, bf16[592,1536]{1,0:T(8,128)(2,1)}, u32[]{:S(2)}, u32[]{:S(2)}) %collective-permute-start.11) | collective-permute-done | bytes 1818656 | tf_op jit(solution)/shard_map/ppermute | solution.py:292
  189.5 38.1 %collective-permute-done.17 = bf16[592,1536]{1,0:T(8,128)(2,1)} collective-permute-done((bf16[592,1536]{1,0:T(8,128)(2,1)}, bf16[592,1536]{1,0:T(8,128)(2,1)}, u32[]{:S(2)}, u32[]{:S(2)}) %collective-permute-start.17) | collective-permute-done | bytes 1818656 | tf_op jit(solution)/shard_map/ppermute | solution.py:292
  246.8 23.0 %attend_forward.2 = (bf16[1024,384]{1,0:T(8,128)(2,1)S(1)}, bf16[160,384]{1,0:T(8,128)(2,1)S(1)}, f32[3,2,1280]{2,1,0:T(2,128)S(1)}) custom-call(s32[2]{0:T(128)S(1)} %pad_add_fusion.length_ref, bf16[1024,1152]{1,0:T(8,128)(2,1)S(1)} %convolution_convert_fusion.1.qi.ki.vi, bf16[1024,1152]{1,0:T(8,128)(2,1)S(1)} %convolution_convert_fusion.1.qi.ki.vi, ...), custom_call_target="tpu_custom_call" | custom-call | flops 10066329600 | bytes 3932160 | tf_op jit(solution)/shard_map/attend_forward/pallas_call | solution.py:173
  293.4 23.0 %attend_forward.3 = (bf16[1024,384]{1,0:T(8,128)(2,1)S(1)}, bf16[160,384]{1,0:T(8,128)(2,1)S(1)}, f32[3,2,1280]{2,1,0:T(2,128)S(1)}) custom-call(s32[2]{0:T(128)S(1)} %pad_add_fusion.length_ref, bf16[1024,1152]{1,0:T(8,128)(2,1)S(1)} %convolution_convert_fusion.qi.ki.vi, bf16[1024,1152]{1,0:T(8,128)(2,1)S(1)} %convolution_convert_fusion.qi.ki.vi, ...), custom_call_target="tpu_custom_call" | custom-call | flops 10066329600 | bytes 3932160 | tf_op jit(solution)/shard_map/attend_forward/pallas_call | solution.py:173
  316.4 15.4 %collective-permute-done.19 = bf16[592,1536]{1,0:T(8,128)(2,1)S(1)} collective-permute-done((bf16[592,1536]{1,0:T(8,128)(2,1)}, bf16[592,1536]{1,0:T(8,128)(2,1)S(1)}, u32[]{:S(2)}, u32[]{:S(2)}) %collective-permute-start.19) | collective-permute-done | bytes 1818656 | tf_op jit(solution)/shard_map/ppermute | solution.py:292
  355.6 12.6 %all-gather.6.cloned.1.call-done = bf16[1536,3072]{1,0:T(8,128)(2,1)} async-done(((bf16[192,3072]{1,0:T(8,128)(2,1)}), bf16[1536,3072]{1,0:T(8,128)(2,1)}) %all-gather.6.cloned.1.call-update) | async-done | bytes 9437200 | tf_op jit(solution)/shard_map/all_gather | solution.py:346
  368.2 12.0 %fusion.20 = (bf16[1024,1536]{1,0:T(8,128)(2,1)}, bf16[1024,1536]{1,0:T(8,128)(2,1)S(1)}) fusion(bf16[1536,3072]{1,0:T(8,128)(2,1)} %all-gather.6.cloned.1.call-done, bf16[1184,1536]{1,0:T(8,128)(2,1)} %maximum_select_fusion.4), kind=kOutput, calls=%fused_computation.70 | convolution fusion | flops 4863295488 | bytes 14155776 | tf_op jit(solution)/shard_map/dot_general | solution.py:28
  411.9 9.3 fusion.26
  430.6 10.1 add_convert_fusion.2
  440.7 10.1 add_convert_fusion.1
  450.8 56.4 %all-gather.8.cloned.1.call-done = bf16[1536,3072]{1,0:T(8,128)(2,1)} async-done(((bf16[192,3072]{1,0:T(8,128)(2,1)}), bf16[1536,3072]{1,0:T(8,128)(2,1)}) %all-gather.8.cloned.1.call-update) | async-done | bytes 9437200 | tf_op jit(solution)/shard_map/all_gather | solution.py:346
  507.3 9.2 pad_maximum_fusion.2
  587.9 10.3 fusion.117
  602.3 8.8 add_convert_fusion
  614.1 11.8 %collective-permute-done.29 = bf16[592,1536]{1,0:T(8,128)(2,1)S(1)} collective-permute-done((bf16[592,1536]{1,0:T(8,128)(2,1)}, bf16[592,1536]{1,0:T(8,128)(2,1)S(1)}, u32[]{:S(2)}, u32[]{:S(2)}) %collective-permute-start.29) | collective-permute-done | bytes 1818656 | tf_op jit(solution)/shard_map/ppermute | solution.py:292
  655.0 42.9 %attend_backward.2 = (bf16[1024,1152]{1,0:T(8,128)(2,1)S(1)}, bf16[160,1152]{1,0:T(8,128)(2,1)S(1)}) custom-call(s32[2]{0:T(128)S(1)} %copy-done.9, bf16[1024,1152]{1,0:T(8,128)(2,1)} %copy-done.17, bf16[1024,1152]{1,0:T(8,128)(2,1)} %copy-done.17, bf16[1024,1152]{1,0:T(8,128)(2,1)} %copy-done.17, bf16[1024,384]{1,0:T(8,128)(2,1)S(1)} %fusion.154.di, ...), custom_call_target="tpu_custom_call" | custom-call | flops 25165824000 | bytes 7864320 | tf_op jit(solution)/shard_map/attend_backward/pallas_call | solution.py:213
  719.9 42.8 %attend_backward.3 = (bf16[1024,1152]{1,0:T(8,128)(2,1)S(1)}, bf16[160,1152]{1,0:T(8,128)(2,1)S(1)}) custom-call(s32[2]{0:T(128)S(1)} %copy-done.9, bf16[1024,1152]{1,0:T(8,128)(2,1)} %copy-done.16, bf16[1024,1152]{1,0:T(8,128)(2,1)} %copy-done.16, bf16[1024,1152]{1,0:T(8,128)(2,1)} %copy-done.16, bf16[1024,384]{1,0:T(8,128)(2,1)S(1)} %fusion.157.di, ...), custom_call_target="tpu_custom_call" | custom-call | flops 25165824000 | bytes 7864320 | tf_op jit(solution)/shard_map/attend_backward/pallas_call | solution.py:213
  836.5 32.6 %collective-permute-done.37 = bf16[592,1536]{1,0:T(8,128)(2,1)} collective-permute-done((bf16[592,1536]{1,0:T(8,128)(2,1)}, bf16[592,1536]{1,0:T(8,128)(2,1)}, u32[]{:S(2)}, u32[]{:S(2)}) %collective-permute-start.37) | collective-permute-done | bytes 1818656 | tf_op jit(solution)/shard_map/ppermute | solution.py:292
  890.4 10.0 collective-permute-done.41
  930.5 10.1 multiply_add_fusion.2
  971.0 41.6 %reduce-scatter.4.cloned.1.call-done = bf16[192,3072]{1,0:T(8,128)(2,1)} async-done(((bf16[1536,3072]{1,0:T(8,128)(2,1)}), bf16[192,3072]{1,0:T(8,128)(2,1)}) %reduce-scatter.4.cloned.1.call-update) | async-done | bytes 1179664 | tf_op jit(solution)/shard_map/reduce_scatter | solution.py:359
  (577 shorter events, 535.7 us)
Async XLA Ops:
  7.2 229.1 %all-gather.4.cloned.1.call-start = ((), (), s32[]{:S(2)}) async-start(), calls=%async_computation.3 | async-start | bytes 10616832 | tf_op jit(solution)/shard_map/all_gather | solution.py:346
  35.6 332.6 %all-gather.6.cloned.1.call-start = ((), (), s32[]{:S(2)}) async-start(), calls=%async_computation.4 | async-start | bytes 10616832 | tf_op jit(solution)/shard_map/all_gather | solution.py:346
  35.7 48.7 %collective-permute-start.13 = (bf16[592,1536]{1,0:T(8,128)(2,1)S(1)}, bf16[592,1536]{1,0:T(8,128)(2,1)}, u32[]{:S(2)}, u32[]{:S(2)}) collective-permute-start(bf16[592,1536]{1,0:T(8,128)(2,1)S(1)} %bitcast.189), channel_id=1, source_target_pairs={{0,1},{1,0},{2,3},{3,2},{4,5},{5,4},{6,7},{7,6},{8,9},{9,8},{10,11... | collective-permute-start | bytes 5455880 | tf_op jit(solution)/shard_map/ppermute | solution.py:257
  80.3 149.6 %collective-permute-start.20 = (bf16[592,1536]{1,0:T(8,128)(2,1)}, bf16[592,1536]{1,0:T(8,128)(2,1)}, u32[]{:S(2)}, u32[]{:S(2)}) collective-permute-start(bf16[592,1536]{1,0:T(8,128)(2,1)} %bitcast.18), channel_id=1, source_target_pairs={{0,1},{1,0},{2,3},{3,2},{4,5},{5,4},{6,7},{7,6},{8,9},{9,8},{10,11... | collective-permute-start | bytes 5455880 | tf_op jit(solution)/shard_map/ppermute | solution.py:257
  80.3 42.7 %collective-permute-start.11 = (bf16[592,1536]{1,0:T(8,128)(2,1)S(1)}, bf16[592,1536]{1,0:T(8,128)(2,1)}, u32[]{:S(2)}, u32[]{:S(2)}) collective-permute-start(bf16[592,1536]{1,0:T(8,128)(2,1)S(1)} %bitcast.190), channel_id=1, source_target_pairs={{0,2},{2,0},{4,6},{6,4},{8,10},{10,8},{12,14},{14,12},{16,18},{18,... | collective-permute-start | bytes 5455880 | tf_op jit(solution)/shard_map/ppermute | solution.py:292
  123.0 41.4 %collective-permute-start.12 = (f32[2,2,4608]{2,1,0:T(2,128)S(1)}, f32[2,2,4608]{2,1,0:T(2,128)}, u32[]{:S(2)}, u32[]{:S(2)}) collective-permute-start(f32[2,2,4608]{2,1,0:T(2,128)S(1)} %reshape.267), channel_id=1, source_target_pairs={{0,1},{1,0},{2,3},{3,2},{4,5},{5,4},{6,7},{7,6},{8,9},{9,8},{10,11... | collective-permute-start | bytes 221192 | tf_op jit(solution)/shard_map/ppermute | solution.py:257
  123.1 49.0 %collective-permute-start.14 = (bf16[592,1536]{1,0:T(8,128)(2,1)}, bf16[592,1536]{1,0:T(8,128)(2,1)}, u32[]{:S(2)}, u32[]{:S(2)}) collective-permute-start(bf16[592,1536]{1,0:T(8,128)(2,1)} %collective-permute-done.11), channel_id=1, source_target_pairs={{0,1},{1,0},{2,3},{3,2},{4,5},{5,4},{6,7},{7,6},{8,9},{9,8},{10,11... | collective-permute-start | bytes 5455880 | tf_op jit(solution)/shard_map/ppermute | solution.py:257
  160.3 21.0 %collective-permute-start.15 = (bf16[96,3072]{1,0:T(8,128)(2,1)}, bf16[96,3072]{1,0:T(8,128)(2,1)}, u32[]{:S(2)}, u32[]{:S(2)}) collective-permute-start(bf16[96,3072]{1,0:T(8,128)(2,1)} %bitcast.64), channel_id=1, source_target_pairs={{0,2},{2,0},{4,6},{6,4},{8,10},{10,8},{12,14},{14,12},{16,18},{18,... | collective-permute-start | bytes 1769480 | tf_op jit(solution)/shard_map/ppermute | solution.py:292
  163.1 26.3 %collective-permute-start.16 = (bf16[96,3072]{1,0:T(8,128)(2,1)}, bf16[96,3072]{1,0:T(8,128)(2,1)}, u32[]{:S(2)}, u32[]{:S(2)}) collective-permute-start(bf16[96,3072]{1,0:T(8,128)(2,1)} %bitcast.72), channel_id=1, source_target_pairs={{0,2},{2,0},{4,6},{6,4},{8,10},{10,8},{12,14},{14,12},{16,18},{18,... | collective-permute-start | bytes 1769480 | tf_op jit(solution)/shard_map/ppermute | solution.py:292
  164.4 63.2 %collective-permute-start.17 = (bf16[592,1536]{1,0:T(8,128)(2,1)}, bf16[592,1536]{1,0:T(8,128)(2,1)}, u32[]{:S(2)}, u32[]{:S(2)}) collective-permute-start(bf16[592,1536]{1,0:T(8,128)(2,1)} %bitcast.18), channel_id=1, source_target_pairs={{0,2},{2,0},{4,6},{6,4},{8,10},{10,8},{12,14},{14,12},{16,18},{18,... | collective-permute-start | bytes 5455880 | tf_op jit(solution)/shard_map/ppermute | solution.py:292
  229.8 277.4 %all-gather.8.cloned.1.call-start = ((), (), s32[]{:S(2)}) async-start(), calls=%async_computation.5 | async-start | bytes 10616832 | tf_op jit(solution)/shard_map/all_gather | solution.py:346
  236.3 40.6 %collective-permute-start.21 = (bf16[592,1536]{1,0:T(8,128)(2,1)}, bf16[592,1536]{1,0:T(8,128)(2,1)}, u32[]{:S(2)}, u32[]{:S(2)}) collective-permute-start(bf16[592,1536]{1,0:T(8,128)(2,1)} %collective-permute-done.17), channel_id=1, source_target_pairs={{0,1},{1,0},{2,3},{3,2},{4,5},{5,4},{6,7},{7,6},{8,9},{9,8},{10,11... | collective-permute-start | bytes 5455880 | tf_op jit(solution)/shard_map/ppermute | solution.py:257
  290.0 41.8 %collective-permute-start.19 = (bf16[592,1536]{1,0:T(8,128)(2,1)}, bf16[592,1536]{1,0:T(8,128)(2,1)S(1)}, u32[]{:S(2)}, u32[]{:S(2)}) collective-permute-start(bf16[592,1536]{1,0:T(8,128)(2,1)} %fusion.76), channel_id=1, source_target_pairs={{0,2},{2,0},{4,6},{6,4},{8,10},{10,8},{12,14},{14,12},{16,18},{18,... | collective-permute-start | bytes 5455880 | tf_op jit(solution)/shard_map/ppermute | solution.py:292
  348.8 579.9 %reduce-scatter.8.cloned.1.call-start = ((), (), s32[]{:S(2)}) async-start(), calls=%async_computation.8 | async-start | bytes 10616832 | tf_op jit(solution)/shard_map/reduce_scatter | solution.py:359
  348.9 47.8 %collective-permute-start.24 = (bf16[592,1536]{1,0:T(8,128)(2,1)S(1)}, bf16[592,1536]{1,0:T(8,128)(2,1)}, u32[]{:S(2)}, u32[]{:S(2)}) collective-permute-start(bf16[592,1536]{1,0:T(8,128)(2,1)S(1)} %add_convert_fusion.4), channel_id=1, source_target_pairs={{0,2},{2,0},{4,6},{6,4},{8,10},{10,8},{12,14},{14,12},{16,18},{18,... | collective-permute-start | bytes 5455880 | tf_op jit(solution)/shard_map/ppermute | solution.py:292
  516.5 433.6 %reduce-scatter.6.cloned.1.call-start = ((), (), s32[]{:S(2)}) async-start(), calls=%async_computation.7 | async-start | bytes 10616832 | tf_op jit(solution)/shard_map/reduce_scatter | solution.py:359
  543.7 21.3 %collective-permute-start.26 = (bf16[592,1536]{1,0:T(8,128)(2,1)S(1)}, bf16[592,1536]{1,0:T(8,128)(2,1)S(1)}, u32[]{:S(2)}, u32[]{:S(2)}) collective-permute-start(bf16[592,1536]{1,0:T(8,128)(2,1)S(1)} %fusion.63), channel_id=1, source_target_pairs={{0,1},{1,0},{2,3},{3,2},{4,5},{5,4},{6,7},{7,6},{8,9},{9,8},{10,11... | collective-permute-start | bytes 5455880 | tf_op jit(solution)/shard_map/ppermute | solution.py:257
  554.9 43.3 %collective-permute-start.28 = (bf16[592,1536]{1,0:T(8,128)(2,1)}, bf16[592,1536]{1,0:T(8,128)(2,1)}, u32[]{:S(2)}, u32[]{:S(2)}) collective-permute-start(bf16[592,1536]{1,0:T(8,128)(2,1)} %fusion.54), channel_id=1, source_target_pairs={{0,1},{1,0},{2,3},{3,2},{4,5},{5,4},{6,7},{7,6},{8,9},{9,8},{10,11... | collective-permute-start | bytes 5455880 | tf_op jit(solution)/shard_map/ppermute | solution.py:257
  581.0 30.2 %collective-permute-start.27 = (bf16[592,1536]{1,0:T(8,128)(2,1)}, bf16[592,1536]{1,0:T(8,128)(2,1)}, u32[]{:S(2)}, u32[]{:S(2)}) collective-permute-start(bf16[592,1536]{1,0:T(8,128)(2,1)} %fusion.59), channel_id=1, source_target_pairs={{0,1},{1,0},{2,3},{3,2},{4,5},{5,4},{6,7},{7,6},{8,9},{9,8},{10,11... | collective-permute-start | bytes 5455880 | tf_op jit(solution)/shard_map/ppermute | solution.py:257
  583.8 42.0 %collective-permute-start.29 = (bf16[592,1536]{1,0:T(8,128)(2,1)}, bf16[592,1536]{1,0:T(8,128)(2,1)S(1)}, u32[]{:S(2)}, u32[]{:S(2)}) collective-permute-start(bf16[592,1536]{1,0:T(8,128)(2,1)} %fusion.66), channel_id=1, source_target_pairs={{0,2},{2,0},{4,6},{6,4},{8,10},{10,8},{12,14},{14,12},{16,18},{18,... | collective-permute-start | bytes 5455880 | tf_op jit(solution)/shard_map/ppermute | solution.py:292
  635.7 376.9 %reduce-scatter.4.cloned.1.call-start = ((), (), s32[]{:S(2)}) async-start(), calls=%async_computation.6 | async-start | bytes 10616832 | tf_op jit(solution)/shard_map/reduce_scatter | solution.py:359
  653.4 44.4 %collective-permute-start.31 = (bf16[592,1536]{1,0:T(8,128)(2,1)S(1)}, bf16[592,1536]{1,0:T(8,128)(2,1)S(1)}, u32[]{:S(2)}, u32[]{:S(2)}) collective-permute-start(bf16[592,1536]{1,0:T(8,128)(2,1)S(1)} %get-tuple-element.181), channel_id=1, source_target_pairs={{0,2},{2,0},{4,6},{6,4},{8,10},{10,8},{12,14},{14,12},{16,18},{18,... | collective-permute-start | bytes 5455880 | tf_op jit(solution)/shard_map/ppermute | solution.py:292
  719.5 43.3 %collective-permute-start.33 = (bf16[592,1536]{1,0:T(8,128)(2,1)S(1)}, bf16[592,1536]{1,0:T(8,128)(2,1)}, u32[]{:S(2)}, u32[]{:S(2)}) collective-permute-start(bf16[592,1536]{1,0:T(8,128)(2,1)S(1)} %copy-done.48), channel_id=1, source_target_pairs={{0,2},{2,0},{4,6},{6,4},{8,10},{10,8},{12,14},{14,12},{16,18},{18,... | collective-permute-start | bytes 5455880 | tf_op jit(solution)/shard_map/ppermute | solution.py:292
  826.9 42.1 %collective-permute-start.37 = (bf16[592,1536]{1,0:T(8,128)(2,1)}, bf16[592,1536]{1,0:T(8,128)(2,1)}, u32[]{:S(2)}, u32[]{:S(2)}) collective-permute-start(bf16[592,1536]{1,0:T(8,128)(2,1)} %fusion.52), channel_id=1, source_target_pairs={{0,2},{2,0},{4,6},{6,4},{8,10},{10,8},{12,14},{14,12},{16,18},{18,... | collective-permute-start | bytes 5455880 | tf_op jit(solution)/shard_map/ppermute | solution.py:292
  (142 other events, 2733.6 us)
Sparse Core Ops, SparseCore 0:
  35.7 142.8 all-gather.3
  230.0 138.2 all-gather.5
  371.0 136.2 all-gather.7
  516.6 161.6 reduce-scatter.7
  681.7 162.3 reduce-scatter.5
  847.6 164.9 reduce-scatter.3
